TPU v7x, 32 devices: a whole 2x2x4 slice. The times are simulated.
32 devices in a mesh: query: 2 (over x), ckpt: 2 (over core), mp: 8 (over z, y).
Axes of the slice: x: 2, y: 2, z: 4, core: 2. Of those that a mesh axis runs over, the one named last changes fastest.
Arguments:
- activations: bfloat16 [2, 1280, 5120], P('ckpt', 'query', 'mp'), parts along dimension 1, may hold values from -6 to 6
- cotangents: bfloat16 [2, 1280, 5120], P('ckpt', 'query', 'mp'), parts along dimension 1, may hold values from -6 to 6
- w_in: bfloat16 [2, 5120, 20480], P('ckpt', None, 'mp'), may hold values from -0.078125 to 0.078125
- b_in: bfloat16 [2, 20480], P('ckpt', 'mp'), may hold values from -3 to 3
- w_out: bfloat16 [2, 20480, 5120], P('ckpt', 'mp'), may hold values from -0.0390625 to 0.0390625
- rates: float32 [2], P('ckpt'), may hold values from 0.5 to 2
- proj_in: bfloat16 [64, 5120], P(None, 'mp'), may hold values from -0.078125 to 0.078125
- proj_out: bfloat16 [20480, 64], P('mp'), may hold values from -0.0390625 to 0.0390625
- lengths: int32 [80], P('query'), parts along dimension 0, may hold values from 1 to 16, 400 in all
Outputs:
- influence: float32 [64, 8], P(('query', 'mp')), parts along dimension 0
There are 2 independent parts, one for each index of `query`. A program takes and returns all parts, laid end to end along the dimension named above; an argument that names none is the same for every part. Nothing has to cross between parts.
Inputs may be any that keep to these rules, and one draw needn't show every extreme that they name: The lengths of one part sum to exactly 400; some example has exactly 16.
All inputs are finite; a program needn't handle non-finite values.
Results may differ from a plain program's by a relative error of at most 0.0042.
Values may be sent and summed in bfloat16 or wider, within the bound.
A program may use at most 192 MiB of HBM per device.

v0:
```python
import math

import jax
import jax.numpy as jnp
from jax import lax
from jax.sharding import PartitionSpec as P

NTR = 32
LIVE = 400


def gelu_slope(z):
    return 0.5 * (1.0 + jax.scipy.special.erf(z / math.sqrt(2.0))) + z * jnp.exp(
        -0.5 * z * z
    ) / math.sqrt(2.0 * math.pi)


def body(activations, cotangents, w_in, b_in, w_out, rates, proj_in, proj_out, lengths):
    x_local = activations[0]
    dy_local = cotangents[0]
    w_first = w_in[0]
    w_second = w_out[0]
    bias = b_in[0]
    rate = rates[0]
    examples = lengths.shape[0]
    padded_rows = x_local.shape[0]
    seq = padded_rows // examples
    k_in = proj_in.shape[0]
    k_out = proj_out.shape[1]
    columns = jnp.arange(examples, dtype=jnp.int32)
    ends = jnp.cumsum(lengths)
    starts = ends - lengths
    row_ids = jnp.arange(LIVE, dtype=jnp.int32)
    owner = jnp.sum((row_ids[:, None] >= ends[None, :]).astype(jnp.int32), axis=1)
    belongs = owner[:, None] == columns[None, :]
    start_of = jnp.sum(jnp.where(belongs, starts[None, :], 0), axis=1)
    source = owner * seq + row_ids - start_of
    x_rows = jnp.take(x_local, source, axis=0)
    dy_rows = jnp.take(dy_local, source, axis=0)
    live = jnp.ones((LIVE,), jnp.float32)

    def to_slots(values):
        slots = jnp.zeros((padded_rows, values.shape[1]), jnp.float32).at[source].set(values)
        return slots.reshape(examples, seq, values.shape[1])

    x_piece = lax.all_gather(x_rows, "mp", axis=1, tiled=True)
    map_piece = lax.all_gather(proj_in, "mp", axis=1, tiled=True)
    pre_acc = jnp.dot(x_piece, w_first, preferred_element_type=jnp.float32)
    left_acc = lax.dot_general(
        x_piece, map_piece, (((1,), (1,)), ((), ())), preferred_element_type=jnp.float32
    )
    pre = pre_acc
    left = left_acc
    pre = pre + bias.astype(jnp.float32)
    back = lax.dot_general(
        lax.all_gather(dy_rows, "mp", axis=1, tiled=True),
        w_second,
        (((1,), (1,)), ((), ())),
        preferred_element_type=jnp.float32,
    )
    dpre = (back * gelu_slope(pre)).astype(jnp.bfloat16)
    left = left * live[:, None]
    right = jnp.dot(dpre, proj_out, preferred_element_type=jnp.float32)
    factor = rate / math.sqrt(k_in * k_out)
    left_blocks = to_slots(left)
    right_blocks = to_slots(right)
    grads = jnp.einsum("esi,esj->ije", left_blocks, right_blocks, precision=lax.Precision.HIGHEST)
    grads = grads.reshape(k_in * k_out, examples)
    owned = lax.psum_scatter(grads, "mp", scatter_dimension=0, tiled=True)
    partial_tile = (
        lax.dot_general(
            owned[:, :NTR],
            owned[:, NTR:],
            (((0,), (0,)), ((), ())),
            precision=lax.Precision.HIGHEST,
        )
        * factor
    )
    tile = lax.psum_scatter(partial_tile, "mp", scatter_dimension=0, tiled=True)
    return lax.psum(tile, "ckpt")


def solution(mesh):
    placed = (
        P("ckpt", "query", "mp"),
        P("ckpt", "query", "mp"),
        P("ckpt", None, "mp"),
        P("ckpt", "mp"),
        P("ckpt", "mp", None),
        P("ckpt"),
        P(None, "mp"),
        P("mp", None),
        P("query"),
    )
    return jax.shard_map(
        body, mesh=mesh, in_specs=placed, out_specs=P(("query", "mp"), None), check_vma=False
    )
```

profile of v0, /device:TPU:0, one launch (start us, length us, event | category | flops | bytes accessed | tf_op | source)
XLA Modules:
  0.0 304.1 jit_solution(6399746120487971579)
XLA Ops:
  6.5 0.9 copy.19
  7.5 0.1 reduce
  7.6 0.7 sub.15
  8.3 0.1 select_reduce_fusion
  8.5 2.2 gather_fusion.1
  10.7 2.2 gather_fusion
  13.0 1.2 broadcast_select_fusion
  14.3 0.7 all-gather.3.cloned.1.call-update
  15.1 35.5 %all_gather.11 = bf16[64,5120]{1,0:T(8,128)(2,1)S(1)} all-gather(bf16[64,640]{1,0:T(8,128)(2,1)S(1)} %copy-done.3), channel_id=1, replica_groups=mesh['query'=2,'ckpt'=2,'mp'=8] {'mp'}, dimensions={1}, use_global_device_ids=true | all-gather | bytes 737280 | tf_op jit(solution)/shard_map/all_gather | solution.py:47
  50.6 43.1 %all-gather.5.cloned.1.call-done = bf16[400,5120]{1,0:T(8,128)(2,1)} async-done(((bf16[400,640]{1,0:T(8,128)(2,1)}), bf16[400,5120]{1,0:T(8,128)(2,1)}) %all-gather.5.cloned.1.call-update) | async-done | bytes 4096016 | tf_op jit(solution)/shard_map/all_gather | solution.py:46
  93.7 18.4 %fusion.7 = f32[400,2560]{1,0:T(8,128)} fusion(bf16[400,5120]{1,0:T(8,128)(2,1)} %all-gather.5.cloned.1.call-done, bf16[1,5120,2560]{2,1,0:T(8,128)(2,1)} %param.13, f32[2560]{0:T(1024)S(1)} %convert_reduce_fusion.1), kind=kOutput, calls=%fused_computation.10 | convolution fusion | flops 10486784000 | bytes 34416640 | tf_op jit(solution)/shard_map/dot_general | solution.py:48
  112.0 54.4 %all-gather.3.cloned.1.call-done = bf16[400,5120]{1,0:T(8,128)(2,1)} async-done(((bf16[400,640]{1,0:T(8,128)(2,1)}), bf16[400,5120]{1,0:T(8,128)(2,1)}) %all-gather.3.cloned.1.call-update) | async-done | bytes 4096016 | tf_op jit(solution)/shard_map/all_gather | solution.py:56
  166.4 19.6 %fusion.18 = f32[400,64]{1,0:T(8,128)S(1)} fusion(bf16[2560,64]{0,1:T(8,128)(2,1)S(1)} %copy-done.5, bf16[400,5120]{1,0:T(8,128)(2,1)} %all-gather.3.cloned.1.call-done, bf16[1,2560,5120]{2,1,0:T(8,128)(2,1)} %param.15, f32[400,2560]{1,0:T(8,128)} %fusion.7), kind=kOutput, calls=%fused_computation.16 | convolution fusion | flops 10627072000 | bytes 34836480 | tf_op jit(solution)/shard_map/dot_general | solution.py:63
  186.0 1.7 scatter_custom_fusion
  187.8 3.4 %fusion.38 = f32[400,64]{1,0:T(8,128)S(1)} fusion(bf16[400,5120]{1,0:T(8,128)(2,1)} %all-gather.5.cloned.1.call-done, bf16[64,5120]{1,0:T(8,128)(2,1)S(1)} %all_gather.11), kind=kOutput, calls=%fused_computation.50 | convolution fusion | flops 262144000 | bytes 4853760 | tf_op jit(solution)/shard_map/dot_general | solution.py:49
  191.2 1.6 scatter_custom_fusion.1
  192.8 2.2 convolution_bitcast_fusion
  195.0 0.4 copy.22
  195.4 1.3 reshape.77
  197.4 0.6 dynamic-slice
  198.6 59.8 %reduce-scatter.2.cloned.1.call-done = f32[512,40]{0,1:T(8,128)} async-done(((f32[4096,40]{0,1:T(8,128)}), f32[512,40]{0,1:T(8,128)}) %reduce-scatter.2.cloned.1.call-update) | async-done | bytes 81936 | tf_op jit(solution)/shard_map/reduce_scatter | solution.py:69
  258.4 1.0 convolution_multiply_fusion
  259.4 35.1 %all-reduce = f32[32,8]{1,0:T(8,128)S(1)} all-reduce(f32[32,8]{1,0:T(8,128)S(1)} %convolution_multiply_fusion), channel_id=3, replica_groups=mesh['query'=2,'ckpt'=2,'mp'=8] {'mp'}, use_global_device_ids=true, to_apply=%region_6.8.clone | all-reduce | flops 256 | bytes 2048
  294.6 3.0 psum.7
  (27 shorter events, 0.4 us)
Async XLA Ops:
  6.5 1.9 copy-start
  6.5 4.2 %copy-start.2 = (bf16[1,640,640]{2,1,0:T(8,128)(2,1)S(1)}, bf16[1,640,640]{2,1,0:T(8,128)(2,1)}, u32[]{:S(2)}) copy-start(bf16[1,640,640]{2,1,0:T(8,128)(2,1)} %param.12) | copy-start | bytes 2457604
  6.5 87.1 %all-gather.5.cloned.1.call-start = ((), (), s32[]{:S(2)}) async-start(), calls=%async_computation.2 | async-start | bytes 4608000 | tf_op jit(solution)/shard_map/all_gather | solution.py:46
  10.7 4.3 %copy-start.4 = (bf16[1,2560]{1,0:T(2,128)(2,1)S(1)}, bf16[1,2560]{1,0:T(2,128)(2,1)}, u32[]{:S(2)}) copy-start(bf16[1,2560]{1,0:T(2,128)(2,1)} %param.14) | copy-start | bytes 15364
  10.7 4.4 %copy-start.3 = (bf16[64,640]{1,0:T(8,128)(2,1)S(1)}, bf16[64,640]{1,0:T(8,128)(2,1)}, u32[]{:S(2)}) copy-start(bf16[64,640]{1,0:T(8,128)(2,1)} %param.17) | copy-start | bytes 245764
  14.2 152.2 %all-gather.3.cloned.1.call-start = ((), (), s32[]{:S(2)}) async-start(), calls=%async_computation.1 | async-start | bytes 4608000 | tf_op jit(solution)/shard_map/all_gather | solution.py:56
  15.0 243.4 %reduce-scatter.2.cloned.1.call-start = ((), (), s32[]{:S(2)}) async-start(), calls=%async_computation.3 | async-start | bytes 737280 | tf_op jit(solution)/shard_map/reduce_scatter | solution.py:69
  50.6 115.9 %copy-start.5 = (bf16[2560,64]{0,1:T(8,128)(2,1)S(1)}, bf16[2560,64]{0,1:T(8,128)(2,1)}, u32[]{:S(2)}) copy-start(bf16[2560,64]{0,1:T(8,128)(2,1)} %param.18) | copy-start | bytes 983044
  187.8 109.8 %copy-start.1 = (bf16[1,640,640]{2,1,0:T(8,128)(2,1)S(1)}, bf16[1,640,640]{2,1,0:T(8,128)(2,1)}, u32[]{:S(2)}) copy-start(bf16[1,640,640]{2,1,0:T(8,128)(2,1)} %param.11) | copy-start | bytes 2457604
  191.2 6.2 %copy-start.6 = (u32[32]{0:T(128)S(1)}, u32[32]{0:T(128)}, u32[]{:S(2)}) copy-start(u32[32]{0:T(128)} %constant.46) | copy-start | bytes 388
Sparse Core Ops, SparseCore 0:
  14.3 79.2 all-gather.4
  95.9 70.4 all-gather.2
  196.9 61.4 reduce-scatter.1
where the time goes:
time: 304 us
  waiting for transfers between devices  158 us (52%)
  blocking collectives  73.6 us (24%)
  matrix products  44.6 us (15%)
  between operations  14.6 us (5%)
  local copies, waits for them, and re-layouts  10.9 us (4%)
    reduce_scatter x1, waiting for transfers between devices, body(): owned = lax.psum_scatter(grads, 'mp', scatter_dimension=0, tiled=True)  59.8 us
    all_gather x1, waiting for transfers between devices, body(): lax.all_gather(dy_rows, 'mp', axis=1, tiled=True)  54.4 us
    all_gather x1, waiting for transfers between devices, body(): x_piece = lax.all_gather(x_rows, 'mp', axis=1, tiled=True)  43.1 us
    all_gather x1, blocking collectives, body(): map_piece = lax.all_gather(proj_in, 'mp', axis=1, tiled=True)  35.5 us
    unnamed x1, blocking collectives  35.1 us
    dot_general x1, matrix products, body(): right = jnp.dot(dpre, proj_out, preferred_element_type=jnp.float32)  19.6 us
    dot_general x1, matrix products, body(): pre_acc = jnp.dot(x_piece, w_first, preferred_element_type=jnp.float32)  18.4 us
  transfers between devices with their start and end apart: 3, of which 3 were waited for; matrix products, arithmetic and copies ran while one was open for 6% of the time, Pallas kernels for 0%

commit v1 on v0

--- a/solution.py
+++ b/solution.py
@@ -1,8 +1,11 @@
+import functools
 import math
 
 import jax
 import jax.numpy as jnp
 from jax import lax
+from jax.experimental import pallas as pl
+from jax.experimental.pallas import tpu as pltpu
 from jax.sharding import PartitionSpec as P
 
 NTR = 32
@@ -80,6 +83,351 @@
     return lax.psum(tile, "ckpt")
 
 
+PIECES = (
+    ((0, 1), (1, 1), (0, 0), (2, 1), (2, 0), (3, 1), (3, 0), (1, 0)),
+    ((1, 1), (2, 1), (1, 0), (0, 1), (3, 1), (0, 0), (2, 0), (3, 0)),
+)
+INWARD, OUTWARD, ACROSS = 0, 1, 2
+TILE = 512
+SHARE = 16
+HIGH = lax.Precision.HIGHEST
+
+
+def routes(rank, owner, same, part):
+    out = []
+    if same:
+        if owner <= rank:
+            out.append(INWARD)
+        if rank == 1 and owner >= 1:
+            out.append(OUTWARD)
+        if rank == 0 and not (owner == 1 and part == 1):
+            out.append(ACROSS)
+        if rank == 1 and owner != 0:
+            out.append(ACROSS)
+    elif rank == 0 and owner == 0:
+        out.append(INWARD)
+    return out
+
+
+def fused_kernel(
+    x_ref, dy_ref, w_in, bias_ref, w_out, rate_ref, map_ref, proj_ref, len_ref,
+    out_ref,
+    xs, dys, win_buf, wout_buf, pre, back, maps, right, gram, parts_out, parts_in, tile_out, tile_in,
+    send_sem, recv_sem, w_sem, map_send, map_recv, part_send, part_recv, tile_send, tile_recv,
+):
+    f32, bf16 = jnp.float32, jnp.bfloat16
+    me = lax.axis_index("mp")
+    q = lax.axis_index("query")
+    c = lax.axis_index("ckpt")
+    z = me // 2
+    y = me % 2
+    far = z // 2
+    rank = z + far * (3 - 2 * z)
+    group = q * 2 + c
+    width = x_ref.shape[2]
+    hidden = w_in.shape[2]
+    tiles = hidden // TILE
+    examples = len_ref.shape[1]
+    padded = x_ref.shape[1]
+    seq = padded // examples
+    k_in = map_ref.shape[0]
+    k_out = proj_ref.shape[1]
+    stacks = (xs, dys)
+    cuts = (((0, 208), (208, 208)), ((0, 208), (208, 192)))
+
+    barrier = pltpu.get_barrier_semaphore()
+    for d in range(16):
+        for dc in range(2):
+            if d < 8 and (d or dc):
+                pl.semaphore_signal(
+                    barrier, inc=1,
+                    device_id={"mp": (me + d) % 8, "ckpt": (c + dc) % 2},
+                    device_id_type=pl.DeviceIdType.MESH,
+                )
+    for dc in range(2):
+        pl.semaphore_signal(
+            barrier, inc=1,
+            device_id={"query": 1 - q, "ckpt": (c + dc) % 2},
+            device_id_type=pl.DeviceIdType.MESH,
+        )
+
+    def index_of(owner, same):
+        zz = owner + far * (3 - 2 * owner)
+        return zz * 2 + (y + 1 - same) % 2
+
+    def piece(k):
+        (o0, s0), (o1, s1) = PIECES[0][k], PIECES[1][k]
+        return index_of(o0 + rank * (o1 - o0), s0 + rank * (s1 - s0))
+
+    def weights(array, k):
+        slot = (array * 8 + k) % 3
+        at = pl.multiple_of(piece(k) * width, 128)
+        if array == 0:
+            return pltpu.make_async_copy(
+                w_in.at[0, pl.ds(at, width), :], win_buf.at[slot], w_sem.at[array, slot]
+            )
+        return pltpu.make_async_copy(
+            w_out.at[0, :, pl.ds(at, width)], wout_buf.at[slot], w_sem.at[array, slot]
+        )
+
+    for k in range(2):
+        weights(0, k).start()
+
+    lens = jnp.broadcast_to(len_ref[...].astype(f32), (8, examples)).astype(bf16)
+
+    def spans(count, example_of):
+        e = lax.broadcasted_iota(jnp.int32, (examples, count), 0)
+        t = example_of(lax.broadcasted_iota(jnp.int32, (examples, count), 1))
+        start = jnp.dot(lens, (e < t).astype(f32).astype(bf16), preferred_element_type=f32)
+        size = jnp.dot(lens, (e == t).astype(f32).astype(bf16), preferred_element_type=f32)
+        return start[0:1], size[0:1]
+
+    start, size = spans(padded, lambda t: t // seq)
+    place = (lax.broadcasted_iota(jnp.int32, (1, padded), 1) % seq).astype(f32)
+    target = jnp.where(place < size, start + place, -1.0)
+    rows = lax.broadcasted_iota(jnp.int32, (LIVE, padded), 0).astype(f32)
+    pick = jnp.where(rows == target, 1.0, 0.0).astype(bf16)
+    xs[me, 0:LIVE, :] = jnp.dot(pick, x_ref[0], preferred_element_type=f32).astype(bf16)
+    xs[me, LIVE : LIVE + SHARE, :] = map_ref[pl.ds(pl.multiple_of(group * SHARE, SHARE), SHARE), :]
+
+    pl.semaphore_wait(barrier, 17)
+
+    sgn = 1 - 2 * far
+    targets = ((z + sgn) * 2 + y, (z - sgn) * 2 + y, z * 2 + 1 - y)
+
+    def copy(array, k, part, direction):
+        o = piece(k)
+        first, count = cuts[array][part]
+        there = stacks[array].at[o, pl.ds(first, count), :]
+        return pltpu.make_async_remote_copy(
+            src_ref=there,
+            dst_ref=there,
+            send_sem=send_sem.at[array, k, part, direction],
+            recv_sem=recv_sem.at[array, o, part],
+            device_id={"mp": targets[direction]},
+            device_id_type=pl.DeviceIdType.MESH,
+        )
+
+    def each_route(array, k, do):
+        for part in range(2):
+            for direction in (OUTWARD, INWARD, ACROSS):
+                ranks = [r for r in range(2) if direction in routes(r, *PIECES[r][k], part)]
+                if len(ranks) == 2:
+                    do(array, k, part, direction)
+                elif ranks:
+                    pl.when(rank == ranks[0])(functools.partial(do, array, k, part, direction))
+        if k == 4:
+            pl.when(rank == 1)(functools.partial(do, array, 2, 1, OUTWARD))
+
+    def send(array, k, part, direction):
+        copy(array, k, part, direction).start()
+
+    def sent(array, k, part, direction):
+        copy(array, k, part, direction).wait_send()
+
+    def arrived(array, k):
+        for part in range(2):
+            copy(array, k, part, ACROSS).wait_recv()
+
+    each_route(0, 0, send)
+    dys[me] = jnp.dot(pick, dy_ref[0], preferred_element_type=f32).astype(bf16)
+
+    def accumulate(array, k):
+        o = piece(k)
+        slot = (array * 8 + k) % 3
+
+        @pl.loop(0, tiles)
+        def _(t):
+            cols = pl.ds(pl.multiple_of(t * TILE, TILE), TILE)
+            if array == 0:
+                term = jnp.dot(xs[o, 0:LIVE, :], win_buf[slot, :, cols], preferred_element_type=f32)
+                if k == 0:
+                    pre[:, cols] = term + bias_ref[:, cols].astype(f32)
+                else:
+                    pre[:, cols] += term
+            else:
+                term = lax.dot_general(
+                    dys[o], wout_buf[slot, cols, :], (((1,), (1,)), ((), ())), preferred_element_type=f32
+                )
+                if k == 0:
+                    back[:, cols] = term
+                elif k < 7:
+                    back[:, cols] += term
+                else:
+                    dpre = ((back[:, cols] + term) * pre[:, cols]).astype(bf16)
+                    part = jnp.dot(dpre, proj_ref[cols, :], preferred_element_type=f32)
+                    right[...] += part
+
+    for array in range(2):
+        for k in range(8):
+            if array == 0 and k == 6:
+                each_route(1, 0, send)
+            if k > 0:
+                arrived(array, k)
+                each_route(array, k, send)
+            if array == 0 and k == 7:
+                own = maps.at[group]
+                for peer in range(1, 4):
+                    pltpu.make_async_remote_copy(
+                        src_ref=xs.at[:, pl.ds(LIVE, SHARE), :],
+                        dst_ref=own,
+                        send_sem=map_send.at[peer],
+                        recv_sem=map_recv.at[peer],
+                        device_id={"query": (q + peer // 2) % 2, "ckpt": (c + peer % 2) % 2},
+                        device_id_type=pl.DeviceIdType.MESH,
+                    ).start()
+                maps[group] = xs[:, LIVE : LIVE + SHARE, :]
+            ahead = array * 8 + k + 2
+            if ahead < 16:
+                weights(ahead // 8, ahead % 8).start()
+            weights(array, k).wait()
+            accumulate(array, k)
+            if array == 1 and k < tiles:
+                cols = pl.ds(k * TILE, TILE)
+                pre[:, cols] = gelu_slope_tile(pre[:, cols])
+            if array == 1 and k == 5:
+                right[...] = jnp.zeros_like(right)
+                for peer in range(1, 4):
+                    other = ((q + peer // 2) % 2) * 2 + (c + peer % 2) % 2
+                    pltpu.make_async_remote_copy(
+                        src_ref=xs.at[:, pl.ds(LIVE, SHARE), :],
+                        dst_ref=maps.at[other],
+                        send_sem=map_send.at[peer],
+                        recv_sem=map_recv.at[peer],
+                        device_id={"query": (q + peer // 2) % 2, "ckpt": (c + peer % 2) % 2},
+                        device_id_type=pl.DeviceIdType.MESH,
+                    ).wait()
+                left = jnp.zeros((LIVE, k_in), f32)
+                for o in range(8):
+                    left += lax.dot_general(
+                        xs[o, 0:LIVE, :],
+                        maps[:, o].reshape(k_in, width),
+                        (((1,), (1,)), ((), ())),
+                        preferred_element_type=f32,
+                    )
+                gram[...] = lax.dot_general(
+                    left, left, (((1,), (1,)), ((), ())), precision=HIGH, preferred_element_type=f32
+                )
+                for j in range(8):
+                    each_route(0, j, sent)
+
+    token = lax.broadcasted_iota(jnp.int32, (LIVE, 64), 0).astype(f32)
+    start, size = spans(64, lambda t: jnp.where(t % 8 < 4, t // 8 * 4 + t % 8, -1))
+    train = jnp.where((token >= start) & (token < start + size), 1.0, 0.0)
+    token = lax.broadcasted_iota(jnp.int32, (LIVE, 128), 0).astype(f32)
+    start, size = spans(128, lambda t: t + NTR)
+    test = jnp.where((token >= start) & (token < start + size), 1.0, 0.0)
+
+    parts_out[...] = right[...].T.reshape(8, k_out // 8, LIVE)
+
+    def part_copy(d):
+        return pltpu.make_async_remote_copy(
+            src_ref=parts_out.at[(me + d) % 8],
+            dst_ref=parts_in.at[d],
+            send_sem=part_send.at[d],
+            recv_sem=part_recv.at[d],
+            device_id={"mp": (me + d) % 8},
+            device_id_type=pl.DeviceIdType.MESH,
+        )
+
+    for d in range(1, 8):
+        part_copy(d).start()
+    parts_in[0] = parts_out[me]
+    for j in range(8):
+        each_route(1, j, sent)
+    for d in range(1, 8):
+        part_copy(d).wait_recv()
+    total = jnp.sum(parts_in[...], axis=0)
+    both = gram[...] * jnp.dot(total.T, total, precision=HIGH, preferred_element_type=f32)
+    half = jnp.dot(both, test, precision=HIGH, preferred_element_type=f32)
+    score = jnp.dot(train.T, half, precision=HIGH, preferred_element_type=f32)
+    score = score * (rate_ref[0] / math.sqrt(k_in * k_out))
+    tile_out[...] = score.reshape(8, 8, 128)
+
+    def tile_copy(d, dc):
+        return pltpu.make_async_remote_copy(
+            src_ref=tile_out.at[(me + d) % 8],
+            dst_ref=tile_in.at[d * 2 + dc],
+            send_sem=tile_send.at[d * 2 + dc],
+            recv_sem=tile_recv.at[d * 2 + dc],
+            device_id={"mp": (me + d) % 8, "ckpt": (c + dc) % 2},
+            device_id_type=pl.DeviceIdType.MESH,
+        )
+
+    for d in range(8):
+        for dc in range(2):
+            if d or dc:
+                tile_copy(d, dc).start()
+    tile_in[0] = tile_out[me]
+    for d in range(1, 8):
+        part_copy(d).wait_send()
+    for d in range(8):
+        for dc in range(2):
+            if d or dc:
+                tile_copy(d, dc).wait()
+    out_ref[...] = jnp.sum(tile_in[...], axis=0)[0:4, 0:8]
+
+
+def gelu_slope_tile(z):
+    return 0.5 * (1.0 + lax.erf(z * (1.0 / math.sqrt(2.0)))) + z * jnp.exp(-0.5 * z * z) * (
+        1.0 / math.sqrt(2.0 * math.pi)
+    )
+
+
+def fused(activations, cotangents, w_in, b_in, w_out, rates, proj_in, proj_out, lengths):
+    width = activations.shape[2]
+    hidden = w_in.shape[2]
+    k_in = proj_in.shape[0]
+    k_out = proj_out.shape[1]
+    f32, bf16 = jnp.float32, jnp.bfloat16
+    vmem = pl.BlockSpec(memory_space=pltpu.VMEM)
+    hbm = pl.BlockSpec(memory_space=pl.ANY)
+    smem = pl.BlockSpec(memory_space=pltpu.SMEM)
+    dma = pltpu.SemaphoreType.DMA
+    return pl.pallas_call(
+        fused_kernel,
+        out_shape=jax.ShapeDtypeStruct((4, 8), f32),
+        in_specs=[vmem, vmem, hbm, vmem, hbm, smem, vmem, vmem, vmem],
+        out_specs=vmem,
+        scratch_shapes=[
+            pltpu.VMEM((8, LIVE + SHARE, width), bf16),
+            pltpu.VMEM((8, LIVE, width), bf16),
+            pltpu.VMEM((3, width, hidden), bf16),
+            pltpu.VMEM((3, hidden, width), bf16),
+            pltpu.VMEM((LIVE, hidden), f32),
+            pltpu.VMEM((LIVE, hidden), f32),
+            pltpu.VMEM((4, 8, SHARE, width), bf16),
+            pltpu.VMEM((LIVE, k_out), f32),
+            pltpu.VMEM((LIVE, LIVE), f32),
+            pltpu.VMEM((8, k_out // 8, LIVE), f32),
+            pltpu.VMEM((8, k_out // 8, LIVE), f32),
+            pltpu.VMEM((8, 8, 128), f32),
+            pltpu.VMEM((16, 8, 128), f32),
+            dma((2, 8, 2, 3)),
+            dma((2, 8, 2)),
+            dma((2, 3)),
+            dma((4,)),
+            dma((4,)),
+            dma((8,)),
+            dma((8,)),
+            dma((16,)),
+            dma((16,)),
+        ],
+        compiler_params=pltpu.CompilerParams(
+            collective_id=0, has_side_effects=True, vmem_limit_bytes=60 * 1024 * 1024
+        ),
+        cost_estimate=pl.CostEstimate(
+            flops=4 * LIVE * 8 * width * hidden,
+            bytes_accessed=32 * width * hidden,
+            transcendentals=2 * LIVE * hidden,
+        ),
+        name="influence",
+    )(
+        activations, cotangents, w_in, b_in, w_out, rates, proj_in, proj_out,
+        lengths.reshape(1, lengths.shape[0]),
+    )
+
+
 def solution(mesh):
     placed = (
         P("ckpt", "query", "mp"),
@@ -92,6 +440,11 @@
         P("mp", None),
         P("query"),
     )
+    fits = mesh.shape["mp"] == 8 and mesh.shape["query"] == 2 and mesh.shape["ckpt"] == 2
     return jax.shard_map(
-        body, mesh=mesh, in_specs=placed, out_specs=P(("query", "mp"), None), check_vma=False
-    )
+        fused if fits else body,
+        mesh=mesh,
+        in_specs=placed,
+        out_specs=P(("query", "mp"), None),
+        check_vma=False,
+    )

time: 304 us -> 128 us (0.42)
  waiting for transfers between devices: 158 us -> 0 us
  Pallas kernels: 0 us -> 124 us
  blocking collectives: 73.6 us -> 0 us
  matrix products: 44.6 us -> 0 us
  between operations: 14.6 us -> 0.66 us
  local copies, waits for them, and re-layouts: 10.9 us -> 3.26 us
    pallas_call x0 -> x1, Pallas kernels: none -> 124 us  [fused(): pl.pallas_call(fused_kernel, out_shape=jax.ShapeDtypeStruct((4, 8), f32),...]
    all_gather x2 -> x0, waiting for transfers between devices: 97.5 us -> none  [the longest x1 54.4 us: body(): lax.all_gather(dy_rows, 'mp', axis=1, tiled=True)]
    reduce_scatter x1 -> x0, waiting for transfers between devices: 59.8 us -> none  [body(): owned = lax.psum_scatter(grads, 'mp', scatter_dimension=0, tiled=True)]
    dot_general x5 -> x0, matrix products: 44.6 us -> none  [the longest x1 19.6 us: body(): right = jnp.dot(dpre, proj_out, preferred_element_type=jnp.float32)]
    all_gather x1 -> x0, blocking collectives: 35.5 us -> none  [body(): map_piece = lax.all_gather(proj_in, 'mp', axis=1, tiled=True)]
    unnamed x1 -> x0, blocking collectives: 35.1 us -> none
    gather x2 -> x0, local copies, waits for them, and re-layouts: 4.46 us -> none  [the longest x1 2.23 us: body(): x_rows = jnp.take(x_local, source, axis=0)]
    scatter x2 -> x0, local copies, waits for them, and re-layouts: 3.29 us -> none  [to_slots(): jnp.zeros((padded_rows, values.shape[1]), jnp.float32).at[source]]
  transfers between devices with their start and end apart: 3 -> 0, of which waited for: 3 -> 0; matrix products, arithmetic and copies ran while one was open for 6% -> 0% of each run, Pallas kernels for 0% -> 0%
where the time goes in v1:
time: 128 us; the launch traced here: 127 us
  Pallas kernels  124 us (97%)
  local copies, waits for them, and re-layouts  3.26 us (3%)
    pallas_call x1, Pallas kernels, fused(): pl.pallas_call(fused_kernel, out_shape=jax.ShapeDtypeStruct((4, 8), f32),...  124 us
    unnamed x2, local copies, waits for them, and re-layouts  3.26 us

profile of v1, /device:TPU:0, one launch (start us, length us, event | category | flops | bytes accessed | tf_op | source)
XLA Modules:
  0.0 127.5 jit_solution(1234452287602681888)
XLA Ops:
  0.7 2.1 %copy.10.proj_ref = bf16[2560,64]{1,0:T(8,128)(2,1)} copy(bf16[2560,64]{0,1:T(8,128)(2,1)} %param.16) | data formatting | bytes 655360 | tf_op args[7]
  2.7 123.6 %influence.1 = f32[4,8]{1,0:T(4,128)} custom-call(bf16[1,640,640]{2,1,0:T(8,128)(2,1)} %x_ref.1, bf16[1,640,640]{2,1,0:T(8,128)(2,1)} %dy_ref.1, bf16[1,5120,2560]{2,1,0:T(8,128)(2,1)} %w_in.1, bf16[1,2560]{1,0:T(2,128)(2,1)} %bias_ref.1, bf16[1,2560,5120]{2,1,0:T(8,128)(2,1)} %w_out.1, f32[1]{0:T(128)S(6)} %copy.12.rate_ref, bf16[64,640]{1,0:T(8,128)(2,1)} %map_ref.1, ...), custom_call_target="tpu_custom_call" | custom-call | flops 20971520000 | bytes 52428800 | tf_op jit(solution)/shard_map/influence/pallas_call | solution.py:387
  126.3 1.2 copy.13

commit v2 on v1

--- a/solution.py
+++ b/solution.py
@@ -91,6 +91,7 @@
 TILE = 512
 SHARE = 16
 HIGH = lax.Precision.HIGHEST
+PARTS = 4
 
 
 def routes(rank, owner, same, part):
@@ -100,7 +101,7 @@
             out.append(INWARD)
         if rank == 1 and owner >= 1:
             out.append(OUTWARD)
-        if rank == 0 and not (owner == 1 and part == 1):
+        if rank == 0 and not (owner == 1 and part >= PARTS // 2):
             out.append(ACROSS)
         if rank == 1 and owner != 0:
             out.append(ACROSS)
@@ -112,8 +113,8 @@
 def fused_kernel(
     x_ref, dy_ref, w_in, bias_ref, w_out, rate_ref, map_ref, proj_ref, len_ref,
     out_ref,
-    xs, dys, win_buf, wout_buf, pre, back, maps, right, gram, parts_out, parts_in, tile_out, tile_in,
-    send_sem, recv_sem, w_sem, map_send, map_recv, part_send, part_recv, tile_send, tile_recv,
+    xs, dys, win_buf, wout_buf, pre, back, maps, right, gram, parts_out, parts_in, tile_out, tile_in, dy_buf, proj_buf,
+    load_sem, send_sem, recv_sem, w_sem, map_send, map_recv, part_send, part_recv, tile_send, tile_recv,
 ):
     f32, bf16 = jnp.float32, jnp.bfloat16
     me = lax.axis_index("mp")
@@ -133,7 +134,11 @@
     k_in = map_ref.shape[0]
     k_out = proj_ref.shape[1]
     stacks = (xs, dys)
-    cuts = (((0, 208), (208, 208)), ((0, 208), (208, 192)))
+    cuts = []
+    for stack in stacks:
+        blocks = stack.shape[1] // SHARE
+        edges = [blocks * p // PARTS * SHARE for p in range(PARTS + 1)]
+        cuts.append([(a, b - a) for a, b in zip(edges, edges[1:])])
 
     barrier = pltpu.get_barrier_semaphore()
     for d in range(16):
@@ -170,6 +175,10 @@
             w_out.at[0, :, pl.ds(at, width)], wout_buf.at[slot], w_sem.at[array, slot]
         )
 
+    dy_load = pltpu.make_async_copy(dy_ref.at[0], dy_buf, load_sem.at[0])
+    proj_load = pltpu.make_async_copy(proj_ref, proj_buf, load_sem.at[1])
+    dy_load.start()
+    proj_load.start()
     for k in range(2):
         weights(0, k).start()
 
@@ -208,16 +217,15 @@
             device_id_type=pl.DeviceIdType.MESH,
         )
 
-    def each_route(array, k, do):
-        for part in range(2):
-            for direction in (OUTWARD, INWARD, ACROSS):
-                ranks = [r for r in range(2) if direction in routes(r, *PIECES[r][k], part)]
-                if len(ranks) == 2:
-                    do(array, k, part, direction)
-                elif ranks:
-                    pl.when(rank == ranks[0])(functools.partial(do, array, k, part, direction))
-        if k == 4:
-            pl.when(rank == 1)(functools.partial(do, array, 2, 1, OUTWARD))
+    def each_route(array, k, part, do):
+        for direction in (OUTWARD, INWARD, ACROSS):
+            ranks = [r for r in range(2) if direction in routes(r, *PIECES[r][k], part)]
+            if len(ranks) == 2:
+                do(array, k, part, direction)
+            elif ranks:
+                pl.when(rank == ranks[0])(functools.partial(do, array, k, part, direction))
+        if k == 4 and part >= PARTS // 2:
+            pl.when(rank == 1)(functools.partial(do, array, 2, part, OUTWARD))
 
     def send(array, k, part, direction):
         copy(array, k, part, direction).start()
@@ -225,12 +233,22 @@
     def sent(array, k, part, direction):
         copy(array, k, part, direction).wait_send()
 
-    def arrived(array, k):
-        for part in range(2):
-            copy(array, k, part, ACROSS).wait_recv()
-
-    each_route(0, 0, send)
-    dys[me] = jnp.dot(pick, dy_ref[0], preferred_element_type=f32).astype(bf16)
+    def pass_on(array, *ks):
+        for part in range(PARTS):
+            for k in ks:
+                if k > 0:
+                    copy(array, k, part, ACROSS).wait_recv()
+                each_route(array, k, part, send)
+
+    def all_sent(array):
+        for k in range(8):
+            for part in range(PARTS):
+                each_route(array, k, part, sent)
+
+    pass_on(0, 0)
+    dy_load.wait()
+    proj_load.wait()
+    dys[me] = jnp.dot(pick, dy_buf[...], preferred_element_type=f32).astype(bf16)
 
     def accumulate(array, k):
         o = piece(k)
@@ -255,16 +273,20 @@
                     back[:, cols] += term
                 else:
                     dpre = ((back[:, cols] + term) * pre[:, cols]).astype(bf16)
-                    part = jnp.dot(dpre, proj_ref[cols, :], preferred_element_type=f32)
+                    part = jnp.dot(dpre, proj_buf[cols, :], preferred_element_type=f32)
                     right[...] += part
 
     for array in range(2):
         for k in range(8):
             if array == 0 and k == 6:
-                each_route(1, 0, send)
-            if k > 0:
-                arrived(array, k)
-                each_route(array, k, send)
+                pass_on(1, 0)
+            if k == 1:
+                pass_on(array, 1, 2)
+                pl.when(rank == 1)(functools.partial(pass_on, array, 3))
+            elif k == 3:
+                pl.when(rank == 0)(functools.partial(pass_on, array, 3))
+            elif k > 3:
+                pass_on(array, k)
             if array == 0 and k == 7:
                 own = maps.at[group]
                 for peer in range(1, 4):
@@ -282,9 +304,11 @@
                 weights(ahead // 8, ahead % 8).start()
             weights(array, k).wait()
             accumulate(array, k)
-            if array == 1 and k < tiles:
-                cols = pl.ds(k * TILE, TILE)
-                pre[:, cols] = gelu_slope_tile(pre[:, cols])
+            if array == 1 and k in (0, 2, 3, 4):
+                first = (0, 0, tiles - 3, tiles - 2, tiles - 1)[k]
+                for t in range(first, first + 1 if k else tiles - 3):
+                    cols = pl.ds(t * TILE, TILE)
+                    pre[:, cols] = gelu_slope_tile(pre[:, cols])
             if array == 1 and k == 5:
                 right[...] = jnp.zeros_like(right)
                 for peer in range(1, 4):
@@ -308,8 +332,7 @@
                 gram[...] = lax.dot_general(
                     left, left, (((1,), (1,)), ((), ())), precision=HIGH, preferred_element_type=f32
                 )
-                for j in range(8):
-                    each_route(0, j, sent)
+                all_sent(0)
 
     token = lax.broadcasted_iota(jnp.int32, (LIVE, 64), 0).astype(f32)
     start, size = spans(64, lambda t: jnp.where(t % 8 < 4, t // 8 * 4 + t % 8, -1))
@@ -333,8 +356,7 @@
     for d in range(1, 8):
         part_copy(d).start()
     parts_in[0] = parts_out[me]
-    for j in range(8):
-        each_route(1, j, sent)
+    all_sent(1)
     for d in range(1, 8):
         part_copy(d).wait_recv()
     total = jnp.sum(parts_in[...], axis=0)
@@ -387,7 +409,7 @@
     return pl.pallas_call(
         fused_kernel,
         out_shape=jax.ShapeDtypeStruct((4, 8), f32),
-        in_specs=[vmem, vmem, hbm, vmem, hbm, smem, vmem, vmem, vmem],
+        in_specs=[vmem, hbm, hbm, vmem, hbm, smem, vmem, hbm, vmem],
         out_specs=vmem,
         scratch_shapes=[
             pltpu.VMEM((8, LIVE + SHARE, width), bf16),
@@ -403,8 +425,11 @@
             pltpu.VMEM((8, k_out // 8, LIVE), f32),
             pltpu.VMEM((8, 8, 128), f32),
             pltpu.VMEM((16, 8, 128), f32),
-            dma((2, 8, 2, 3)),
-            dma((2, 8, 2)),
+            pltpu.VMEM(cotangents.shape[1:], bf16),
+            pltpu.VMEM(proj_out.shape, bf16),
+            dma((2,)),
+            dma((2, 8, PARTS, 3)),
+            dma((2, 8, PARTS)),
             dma((2, 3)),
             dma((4,)),
             dma((4,)),

time: 128 us -> 117 us (0.914)
  Pallas kernels: 124 us -> 113 us
    pallas_call x1, Pallas kernels: 124 us -> 113 us  [fused(): pl.pallas_call(fused_kernel, out_shape=jax.ShapeDtypeStruct((4, 8), f32),...]
where the time goes in v2:
time: 117 us
  Pallas kernels  113 us (97%)
  local copies, waits for them, and re-layouts  3.26 us (3%)
    pallas_call x1, Pallas kernels, fused(): pl.pallas_call(fused_kernel, out_shape=jax.ShapeDtypeStruct((4, 8), f32),...  113 us
    unnamed x2, local copies, waits for them, and re-layouts  3.26 us

profile of v2, /device:TPU:0, one launch (start us, length us, event | category | flops | bytes accessed | tf_op | source)
XLA Modules:
  0.0 116.9 jit_solution(12228870029590561155)
XLA Ops:
  0.7 2.1 %copy.10.proj_ref = bf16[2560,64]{1,0:T(8,128)(2,1)} copy(bf16[2560,64]{0,1:T(8,128)(2,1)} %param.16) | data formatting | bytes 655360 | tf_op args[7]
  2.7 113.0 %influence.1 = f32[4,8]{1,0:T(4,128)} custom-call(bf16[1,640,640]{2,1,0:T(8,128)(2,1)} %x_ref.1, bf16[1,640,640]{2,1,0:T(8,128)(2,1)} %dy_ref.1, bf16[1,5120,2560]{2,1,0:T(8,128)(2,1)} %w_in.1, bf16[1,2560]{1,0:T(2,128)(2,1)} %bias_ref.1, bf16[1,2560,5120]{2,1,0:T(8,128)(2,1)} %w_out.1, f32[1]{0:T(128)S(6)} %copy.12.rate_ref, bf16[64,640]{1,0:T(8,128)(2,1)} %map_ref.1, ...), custom_call_target="tpu_custom_call" | custom-call | flops 20971520000 | bytes 52428800 | tf_op jit(solution)/shard_map/influence/pallas_call | solution.py:409
  115.7 1.2 %copy.13 = f32[4,8]{1,0:T(4,128)} copy(f32[4,8]{1,0:T(4,128)} %influence.1) | data formatting | bytes 256

commit v3 on v2

--- a/solution.py
+++ b/solution.py
@@ -113,7 +113,7 @@
 def fused_kernel(
     x_ref, dy_ref, w_in, bias_ref, w_out, rate_ref, map_ref, proj_ref, len_ref,
     out_ref,
-    xs, dys, win_buf, wout_buf, pre, back, maps, right, gram, parts_out, parts_in, tile_out, tile_in, dy_buf, proj_buf,
+    xs, dys, win_buf, wout_buf, pre, back, maps, right, gram, parts_out, parts_in, tile_out, tile_in, dy_buf, proj_buf, train, test,
     load_sem, send_sem, recv_sem, w_sem, map_send, map_recv, part_send, part_recv, tile_send, tile_recv,
 ):
     f32, bf16 = jnp.float32, jnp.bfloat16
@@ -131,6 +131,7 @@
     examples = len_ref.shape[1]
     padded = x_ref.shape[1]
     seq = padded // examples
+    last = gram.shape[1]
     k_in = map_ref.shape[0]
     k_out = proj_ref.shape[1]
     stacks = (xs, dys)
@@ -329,17 +330,17 @@
                         (((1,), (1,)), ((), ())),
                         preferred_element_type=f32,
                     )
+                first = LIVE - last
                 gram[...] = lax.dot_general(
-                    left, left, (((1,), (1,)), ((), ())), precision=HIGH, preferred_element_type=f32
+                    left, left[first:], (((1,), (1,)), ((), ())), precision=HIGH, preferred_element_type=f32
                 )
+                token = lax.broadcasted_iota(jnp.int32, (LIVE, 64), 0).astype(f32)
+                start, size = spans(64, lambda t: jnp.where(t % 8 < 4, t // 8 * 4 + t % 8, -1))
+                train[...] = jnp.where((token >= start) & (token < start + size), 1.0, 0.0).T
+                token = lax.broadcasted_iota(jnp.int32, (last, 128), 0).astype(f32) + first
+                start, size = spans(128, lambda t: t + NTR)
+                test[...] = jnp.where((token >= start) & (token < start + size), 1.0, 0.0)
                 all_sent(0)
-
-    token = lax.broadcasted_iota(jnp.int32, (LIVE, 64), 0).astype(f32)
-    start, size = spans(64, lambda t: jnp.where(t % 8 < 4, t // 8 * 4 + t % 8, -1))
-    train = jnp.where((token >= start) & (token < start + size), 1.0, 0.0)
-    token = lax.broadcasted_iota(jnp.int32, (LIVE, 128), 0).astype(f32)
-    start, size = spans(128, lambda t: t + NTR)
-    test = jnp.where((token >= start) & (token < start + size), 1.0, 0.0)
 
     parts_out[...] = right[...].T.reshape(8, k_out // 8, LIVE)
 
@@ -360,9 +361,12 @@
     for d in range(1, 8):
         part_copy(d).wait_recv()
     total = jnp.sum(parts_in[...], axis=0)
-    both = gram[...] * jnp.dot(total.T, total, precision=HIGH, preferred_element_type=f32)
-    half = jnp.dot(both, test, precision=HIGH, preferred_element_type=f32)
-    score = jnp.dot(train.T, half, precision=HIGH, preferred_element_type=f32)
+    total = total.T
+    both = gram[...] * lax.dot_general(
+        total, total[LIVE - last :], (((1,), (1,)), ((), ())), precision=HIGH, preferred_element_type=f32
+    )
+    half = jnp.dot(both, test[...], precision=HIGH, preferred_element_type=f32)
+    score = jnp.dot(train[...], half, precision=HIGH, preferred_element_type=f32)
     score = score * (rate_ref[0] / math.sqrt(k_in * k_out))
     tile_out[...] = score.reshape(8, 8, 128)
 
@@ -401,6 +405,8 @@
     hidden = w_in.shape[2]
     k_in = proj_in.shape[0]
     k_out = proj_out.shape[1]
+    examples = lengths.shape[0]
+    last = activations.shape[1] // examples * (examples - NTR)
     f32, bf16 = jnp.float32, jnp.bfloat16
     vmem = pl.BlockSpec(memory_space=pltpu.VMEM)
     hbm = pl.BlockSpec(memory_space=pl.ANY)
@@ -420,13 +426,15 @@
             pltpu.VMEM((LIVE, hidden), f32),
             pltpu.VMEM((4, 8, SHARE, width), bf16),
             pltpu.VMEM((LIVE, k_out), f32),
-            pltpu.VMEM((LIVE, LIVE), f32),
+            pltpu.VMEM((LIVE, last), f32),
             pltpu.VMEM((8, k_out // 8, LIVE), f32),
             pltpu.VMEM((8, k_out // 8, LIVE), f32),
             pltpu.VMEM((8, 8, 128), f32),
             pltpu.VMEM((16, 8, 128), f32),
             pltpu.VMEM(cotangents.shape[1:], bf16),
             pltpu.VMEM(proj_out.shape, bf16),
+            pltpu.VMEM((64, LIVE), f32),
+            pltpu.VMEM((last, 128), f32),
             dma((2,)),
             dma((2, 8, PARTS, 3)),
             dma((2, 8, PARTS)),

time: 117 us -> 116 us (level)
  no operation moved by 1% of the time
where the time goes in v3:
time: 116 us
  Pallas kernels  112 us (97%)
  local copies, waits for them, and re-layouts  3.26 us (3%)
    pallas_call x1, Pallas kernels, fused(): pl.pallas_call(fused_kernel, out_shape=jax.ShapeDtypeStruct((4, 8), f32),...  112 us
    unnamed x2, local copies, waits for them, and re-layouts  3.26 us

profile of v3, /device:TPU:0, one launch (start us, length us, event | category | flops | bytes accessed | tf_op | source)
XLA Modules:
  0.0 115.9 jit_solution(15361053264926164717)
XLA Ops:
  0.7 2.1 %copy.10.proj_ref = bf16[2560,64]{1,0:T(8,128)(2,1)} copy(bf16[2560,64]{0,1:T(8,128)(2,1)} %param.16) | data formatting | bytes 655360 | tf_op args[7]
  2.7 111.9 %influence.1 = f32[4,8]{1,0:T(4,128)} custom-call(bf16[1,640,640]{2,1,0:T(8,128)(2,1)} %x_ref.1, bf16[1,640,640]{2,1,0:T(8,128)(2,1)} %dy_ref.1, bf16[1,5120,2560]{2,1,0:T(8,128)(2,1)} %w_in.1, bf16[1,2560]{1,0:T(2,128)(2,1)} %bias_ref.1, bf16[1,2560,5120]{2,1,0:T(8,128)(2,1)} %w_out.1, f32[1]{0:T(128)S(6)} %copy.12.rate_ref, bf16[64,640]{1,0:T(8,128)(2,1)} %map_ref.1, ...), custom_call_target="tpu_custom_call" | custom-call | flops 20971520000 | bytes 52428800 | tf_op jit(solution)/shard_map/influence/pallas_call | solution.py:415
  114.7 1.2 %copy.13 = f32[4,8]{1,0:T(4,128)} copy(f32[4,8]{1,0:T(4,128)} %influence.1) | data formatting | bytes 256
